TPU v7x, 256 devices: a whole 4x4x8 slice. The times are simulated.
256 devices in a mesh: grp: 32 (over z, y), tp: 8 (over x, core).
Axes of the slice: x: 4, y: 4, z: 8, core: 2. Of those that a mesh axis runs over, the one named last changes fastest.
Arguments:
- hidden: bfloat16 [8192, 7168], P('grp', 'tp'), may hold values from -6 to 6
- w_dkv: bfloat16 [7168, 576], P('tp'), may hold values from -0.0625 to 0.0625
- kv_gain: float32 [512], replicated, may hold values from 0.1 to 1.9
- queries: bfloat16 [8192, 24576], P('grp', 'tp'), may hold values from -18 to 18
- w_uk: bfloat16 [512, 16384], P(None, 'tp'), may hold values from -0.5 to 0.5
- w_uv: bfloat16 [512, 16384], P(None, 'tp'), may hold values from -0.25 to 0.25
- store: bfloat16 [1024, 576, 128], P('grp'), may hold values from -18 to 18
- page_table: int32 [128, 8], replicated, may hold values from 0 to 1023, as said below
- cached_len: int32 [128], replicated, may hold values from 512 to 1024
- app_len: int32 [128], replicated, may hold values from 16 to 64
Outputs:
- attended: bfloat16 [8192, 16384], P('grp', 'tp')
Inputs may be any that keep to these rules, and one draw needn't show every extreme that they name: `page_table`: every store page is named once. The pages of the trajectories resumed on decode group g (rows g * 4 to (g + 1) * 4 - 1) lie exactly 1 in each block of 32 store pages.
All inputs are finite; a program needn't handle non-finite values.
Results may differ from a plain program's by a relative error of at most 0.0072.
Values may be sent and summed in bfloat16 or wider, within the bound.
A program may use at most 128 MiB of HBM per device.

v0:
```python
import math

import jax
import jax.numpy as jnp
from jax import lax
from jax.sharding import PartitionSpec as P

NOPE = 128
ROPE = 64
LAT = 512
VHEAD = 128
PAGE = 128
MAXP = 8
TR_G = 4
APP = 64


def angle_table(positions, width):
    half = width // 2
    freq = jnp.exp(jnp.arange(half).astype(jnp.float32) * (-2.0 * math.log(10000.0) / width))
    return positions.astype(jnp.float32)[:, None] * freq[None, :]


def rotate(vec, angles):
    half = vec.shape[-1] // 2
    first = vec[..., :half]
    second = vec[..., half:]
    cosine = jnp.cos(angles)
    sine = jnp.sin(angles)
    return jnp.concatenate(
        [first * cosine - second * sine, first * sine + second * cosine], axis=-1
    )


def finish_keys(kv, positions, kv_gain, lat_width):
    latent = kv[:, :lat_width]
    factor = lax.rsqrt(jnp.mean(latent * latent, axis=-1, keepdims=True) + 1e-06)
    latent = latent * factor * kv_gain[None, :]
    rotary = rotate(kv[:, lat_width:], angle_table(positions, kv.shape[1] - lat_width))
    return jnp.concatenate([latent, rotary], axis=-1).astype(jnp.bfloat16)


def attend_local(q_full, pages, fresh, length, count, w_uv3):
    rows = q_full.shape[0]
    factor = 1.0 / math.sqrt(NOPE + ROPE)
    older = jnp.einsum("qhc,mcp->hqmp", q_full, pages, preferred_element_type=jnp.float32) * factor
    older = older.reshape(older.shape[0], rows, -1)
    spots = jnp.arange(older.shape[-1], dtype=jnp.int32)
    older = jnp.where((spots < length)[None, None, :], older, -jnp.inf)
    newer = jnp.einsum("qhc,kc->hqk", q_full, fresh, preferred_element_type=jnp.float32) * factor
    slots = jnp.arange(rows, dtype=jnp.int32)
    allowed = (slots[None, :] <= slots[:, None]) & (slots[None, :] < count)
    newer = jnp.where(allowed[None], newer, -jnp.inf)
    top = jnp.maximum(
        jnp.max(older, axis=-1, keepdims=True), jnp.max(newer, axis=-1, keepdims=True)
    )
    exp_old = jnp.exp(older - top)
    exp_new = jnp.exp(newer - top)
    total = jnp.sum(exp_old, axis=-1, keepdims=True) + jnp.sum(exp_new, axis=-1, keepdims=True)
    prob_old = (exp_old / total).astype(jnp.bfloat16).reshape(older.shape[0], rows, MAXP, PAGE)
    prob_new = (exp_new / total).astype(jnp.bfloat16)
    o_lat = jnp.einsum(
        "hqmp,mcp->qhc", prob_old, pages[:, :LAT, :], preferred_element_type=jnp.float32
    )
    o_lat = o_lat + jnp.einsum(
        "hqk,kc->qhc", prob_new, fresh[:, :LAT], preferred_element_type=jnp.float32
    )
    o_lat = o_lat.astype(jnp.bfloat16)
    out = jnp.einsum("qhc,chv->qhv", o_lat, w_uv3, preferred_element_type=jnp.float32)
    out = jnp.where((slots < count)[:, None, None], out, 0.0)
    return out.reshape(rows, -1).astype(jnp.bfloat16)


def body(hidden, w_dkv, kv_gain, queries, w_uk, w_uv, store, page_table, cached_len, app_len):
    group = lax.axis_index("grp")
    groups = lax.axis_size("grp")
    per_group = store.shape[0]
    heads = w_uk.shape[1] // NOPE
    entries = page_table.shape[0] * page_table.shape[1]
    flat = page_table.reshape(-1)
    counter = jnp.arange(entries, dtype=jnp.int32)
    source = flat // per_group
    target = counter // (MAXP * TR_G)
    sort_keys = jnp.where(source == group, target * entries + counter, groups * entries + counter)
    send_order = jnp.argsort(sort_keys)[:per_group]
    send_slots = flat[send_order] - group * per_group
    own = lax.dynamic_slice_in_dim(flat, group * per_group, per_group, 0)
    own_counter = jnp.arange(per_group, dtype=jnp.int32)
    recv_order = jnp.argsort(own // per_group * per_group + own_counter)
    placing = jnp.argsort(recv_order)
    arrived = lax.all_to_all(store[send_slots], "grp", split_axis=0, concat_axis=0, tiled=True)
    pages = arrived[placing].reshape(TR_G, MAXP, store.shape[1], store.shape[2])
    lengths = lax.dynamic_slice_in_dim(cached_len, group * TR_G, TR_G, 0)
    counts = lax.dynamic_slice_in_dim(app_len, group * TR_G, TR_G, 0)
    positions = (lengths[:, None] + jnp.arange(APP, dtype=jnp.int32)[None, :]).reshape(-1)
    partial_value = jnp.dot(hidden, w_dkv, preferred_element_type=jnp.float32)
    fresh_all = finish_keys(lax.psum(partial_value, "tp"), positions, kv_gain, LAT)
    q = queries.reshape(queries.shape[0], heads, NOPE + ROPE)
    q_lat = jnp.einsum(
        "qhn,lhn->qhl",
        q[..., :NOPE],
        w_uk.reshape(LAT, heads, NOPE),
        preferred_element_type=jnp.float32,
    ).astype(jnp.bfloat16)
    q_rope = rotate(
        q[..., NOPE:].astype(jnp.float32), angle_table(positions, ROPE)[:, None, :]
    ).astype(jnp.bfloat16)
    q_full = jnp.concatenate([q_lat, q_rope], axis=-1)
    w_uv3 = w_uv.reshape(LAT, heads, VHEAD)
    results = []
    for slot in range(TR_G):
        lo = slot * APP
        results.append(
            attend_local(
                q_full[lo : lo + APP],
                pages[slot],
                fresh_all[lo : lo + APP],
                lengths[slot],
                counts[slot],
                w_uv3,
            )
        )
    return jnp.concatenate(results, axis=0)


def solution(mesh):
    in_specs = (
        P("grp", "tp"),
        P("tp", None),
        P(),
        P("grp", "tp"),
        P(None, "tp"),
        P(None, "tp"),
        P("grp", None, None),
        P(),
        P(),
        P(),
    )
    out_specs = P("grp", "tp")
    return jax.shard_map(body, mesh=mesh, in_specs=in_specs, out_specs=out_specs, check_vma=False)
```

profile of v0, /device:TPU:15, one launch (start us, length us, event | category | flops | bytes accessed | tf_op | source)
XLA Modules:
  0.0 209.8 jit_solution(14768790370730774648)
XLA Ops:
  6.5 0.9 copy.32
  7.6 4.4 %sort.48 = (s32[1024]{0:T(1024)}, s32[1024]{0:T(1024)S(1)}) sort(s32[1024]{0:T(1024)S(1)} %fusion.152, s32[1024]{0:T(1024)S(1)} %iota.148), dimensions={0}, to_apply=%region_0.1 | sort | flops 10240 | bytes 16384 | tf_op jit(solution)/shard_map/jit(argsort)/sort | solution.py:85
  12.0 0.7 gather_fusion
  12.7 5.7 %gather_fusion.1 = bf16[32,576,128]{2,1,0:T(8,128)(2,1)} fusion(bf16[32,576,128]{2,1,0:T(8,128)(2,1)} %param.16, s32[1024]{0:T(1024)S(1)} %pad_clamp_fusion.1), kind=kCustom, calls=%fused_computation.1 | custom fusion | bytes 9437312 | tf_op jit(solution)/shard_map/gather | solution.py:91
  18.3 11.3 %all-to-all-start = ((bf16[32,576,128]{2,1,0:T(8,128)(2,1)}), bf16[32,576,128]{2,1,0:T(8,128)(2,1)}, u32[]{:S(2)}, u32[]{:S(2)}) async-start(bf16[32,576,128]{2,1,0:T(8,128)(2,1)} %gather_fusion.1), calls=%async_computation | async-start | bytes 9437184 | tf_op jit(solution)/shard_map/all_to_all | solution.py:91
  29.7 2.3 %fusion.166 = f32[256,576]{0,1:T(8,128)} fusion(bf16[256,896]{1,0:T(8,128)(2,1)} %param.10, bf16[896,576]{0,1:T(8,128)(2,1)S(1)} %copy-done.7), kind=kOutput, calls=%fused_computation.200 | convolution fusion | flops 264241152 | bytes 2080768 | tf_op jit(solution)/shard_map/dot_general | solution.py:96
  32.1 2.6 %copy.33 = bf16[256,3072]{0,1:T(8,128)(2,1)} copy(bf16[256,3072]{1,0:T(8,128)(2,1)} %param.13) | data formatting | bytes 3145728 | tf_op args[3]
  34.9 1.7 sort.49
  36.6 1.7 sort.50
  39.6 0.7 iota_compare_fusion.3
  40.9 0.7 iota_compare_fusion.1
  41.6 0.7 fusion.161
  42.9 0.7 fusion.155
  44.2 0.7 fusion.153
  45.3 4.6 %convert_bitcast_fusion = bf16[256,16,512]{0,2,1:T(8,128)(2,1)} fusion(bf16[256,16,192]{0,2,1:T(8,128)(2,1)} %bitcast.256, bf16[512,2048]{1,0:T(8,128)(2,1)S(1)} %copy-done), kind=kOutput, calls=%fused_computation.24 | convolution fusion | flops 538968064 | bytes 7340032 | tf_op jit(solution)/shard_map/qhn,lhn->qhl/dot_general | solution.py:99
  50.0 1.2 slice_convert_fusion
  51.1 50.2 %all-reduce.2.cloned.1.call-done = f32[256,576]{0,1:T(8,128)} async-done(((f32[256,576]{0,1:T(8,128)}), f32[256,576]{0,1:T(8,128)}) %all-reduce.2.cloned.1.call-update) | async-done | bytes 589840 | tf_op jit(solution)/shard_map/psum | solution.py:97
  101.3 1.1 multiply_reduce_fusion
  102.4 1.0 subtract_convert_fusion.1
  103.4 1.2 multiply_convert_fusion
  104.8 2.4 %pad_maximum_fusion = bf16[256,16,576]{0,2,1:T(8,128)(2,1)S(1)} fusion(bf16[256,16,32]{0,2,1:T(8,128)(2,1)S(1)} %get-tuple-element.12, bf16[256,16,32]{0,2,1:T(8,128)(2,1)S(1)} %get-tuple-element.11, bf16[256,16,512]{0,2,1:T(8,128)(2,1)} %convert_bitcast_fusion), kind=kLoop, calls=%fused_computation.3 | loop fusion | flops 14155776 | bytes 9437184 | tf_op jit(solution)/shard_map/concatenate | solution.py:108
  107.9 1.9 fusion.164
  110.5 1.1 fusion.162
  111.6 27.1 %all-to-all-done = bf16[32,576,128]{2,1,0:T(8,128)(2,1)} async-done(((bf16[32,576,128]{2,1,0:T(8,128)(2,1)}), bf16[32,576,128]{2,1,0:T(8,128)(2,1)}, u32[]{:S(2)}, u32[]{:S(2)}) %all-to-all-start) | async-done | bytes 4718624 | tf_op jit(solution)/shard_map/all_to_all | solution.py:91
  138.7 5.7 %gather_fusion.2 = bf16[32,576,128]{2,1,0:T(8,128)(2,1)} fusion(bf16[32,576,128]{2,1,0:T(8,128)(2,1)} %all-to-all-done, s32[1024]{0:T(1024)S(1)} %pad_clamp_fusion), kind=kCustom, calls=%fused_computation.2 | custom fusion | bytes 9437312 | tf_op jit(solution)/shard_map/gather | solution.py:92
  144.3 4.0 %bitcast_reduce_fusion.3 = (f32[16,64]{1,0:T(8,128)S(1)}, f32[8,128,64,16]{1,2,3,0:T(8,128)S(1)}) fusion(pred[8,128]{1,0:T(8,128)(4,1)S(1)} %fusion.156, bf16[256,16,576]{0,2,1:T(8,128)(2,1)} %copy-done.2, bf16[32,576,128]{2,1,0:T(8,128)(2,1)} %gather_fusion.2), kind=kOutput, calls=%fused_computation.14 | convolution fusion | flops 1211104256 | bytes 7738368 | tf_op jit(solution)/shard_map/qhc,mcp->hqmp/dot_general | solution.py:46
  148.5 1.0 fusion.4
  149.6 1.4 divide_convert_fusion.3
  151.0 1.2 copy-done.3
  152.1 2.6 %fusion.121 = f32[512,1024,1]{0,1,2:T(8,128)} fusion(bf16[8,128,1024]{1,2,0:T(8,128)(2,1)S(1)} %bitcast.259, bf16[32,576,128]{2,1,0:T(8,128)(2,1)S(1)} %copy-done.3), kind=kOutput, calls=%fused_computation.102 | convolution fusion | flops 1073741824 | bytes 5242880
  154.7 3.0 %bitcast_reduce_fusion.2 = (f32[16,64]{1,0:T(8,128)S(1)}, f32[8,128,64,16]{1,2,3,0:T(8,128)S(1)}) fusion(pred[8,128]{1,0:T(8,128)(4,1)S(1)} %fusion.155, bf16[256,16,576]{0,2,1:T(8,128)(2,1)S(1)} %bitcast.255, bf16[32,576,128]{2,1,0:T(8,128)(2,1)S(1)} %copy-done.3), kind=kOutput, calls=%fused_computation.11 | convolution fusion | flops 1211104256 | bytes 7738368 | tf_op jit(solution)/shard_map/qhc,mcp->hqmp/dot_general | solution.py:46
  157.9 1.0 fusion.5
  158.9 1.2 divide_convert_fusion.2
  160.1 2.6 %fusion.118 = f32[512,1024,1]{0,1,2:T(8,128)} fusion(bf16[8,128,1024]{1,2,0:T(8,128)(2,1)S(1)} %bitcast.260, bf16[32,576,128]{2,1,0:T(8,128)(2,1)S(1)} %copy-done.3), kind=kOutput, calls=%fused_computation.99 | convolution fusion | flops 1073741824 | bytes 5242880
  162.7 4.1 %fusion.102 = bf16[16,8,8,128]{3,2,1,0:T(8,128)(2,1)} fusion(f32[512,16,64]{0,2,1:T(8,128)} %bitcast.262, f32[16,64,64]{1,2,0:T(8,128)} %copy-done.6, f32[16,64]{1,0:T(8,128)S(1)} %add.148, f32[16,64]{1,0:T(8,128)S(1)} %max.32, pred[64]{0:T(512)(128)(4,1)S(1)} %iota_compare_fusion.4, bf16[256,512]{0,1:T(8,128)(2,1)S(1)} %multiply_convert_fusion, ...), kind=kOutput, calls=%fused_computation.91 | convolution fusion | flops 202833920 | bytes 4866560 | tf_op jit(solution)/shard_map/qhc,chv->qhv/dot_general | solution.py:69
  166.9 4.0 %fusion.105 = bf16[16,8,8,128]{3,2,1,0:T(8,128)(2,1)} fusion(f32[512,16,64]{0,2,1:T(8,128)} %bitcast.263, f32[16,64,64]{1,2,0:T(8,128)S(1)} %copy-done.5, f32[16,64]{1,0:T(8,128)S(1)} %add.150, f32[16,64]{1,0:T(8,128)S(1)} %max.33, pred[64]{0:T(512)(128)(4,1)S(1)} %iota_compare_fusion.3, bf16[256,512]{0,1:T(8,128)(2,1)S(1)} %multiply_convert_fusion, ...), kind=kOutput, calls=%fused_computation.92 | convolution fusion | flops 202833920 | bytes 5128704 | tf_op jit(solution)/shard_map/qhc,chv->qhv/dot_general | solution.py:69
  170.8 4.0 %bitcast_reduce_fusion.1 = (f32[16,64]{1,0:T(8,128)S(1)}, f32[8,128,64,16]{1,2,3,0:T(8,128)S(1)}) fusion(pred[8,128]{1,0:T(8,128)(4,1)S(1)} %fusion.154, bf16[256,16,576]{0,2,1:T(8,128)(2,1)} %copy-done.2, bf16[32,576,128]{2,1,0:T(8,128)(2,1)} %gather_fusion.2), kind=kOutput, calls=%fused_computation.8 | convolution fusion | flops 1211104256 | bytes 7738368 | tf_op jit(solution)/shard_map/qhc,mcp->hqmp/dot_general | solution.py:46
  175.0 1.0 fusion.6
  176.0 1.4 divide_convert_fusion.1
  177.5 3.9 %fusion.116 = f32[512,1024,1]{0,1,2:T(8,128)} fusion(bf16[8,128,1024]{1,2,0:T(8,128)(2,1)S(1)} %bitcast.261, bf16[32,576,128]{2,1,0:T(8,128)(2,1)} %gather_fusion.2), kind=kOutput, calls=%fused_computation.97 | convolution fusion | flops 1073741824 | bytes 5242880
  181.3 4.0 %fusion.108 = bf16[16,8,8,128]{3,2,1,0:T(8,128)(2,1)} fusion(f32[512,16,64]{0,2,1:T(8,128)} %bitcast.265, f32[16,64,64]{1,2,0:T(8,128)S(1)} %get-tuple-element.32, f32[16,64]{1,0:T(8,128)S(1)} %add.152, f32[16,64]{1,0:T(8,128)S(1)} %max.34, pred[64]{0:T(512)(128)(4,1)S(1)} %iota_compare_fusion.2, bf16[256,512]{0,1:T(8,128)(2,1)S(1)} %multiply_convert_fusion, ...), kind=kOutput, calls=%fused_computation.93 | convolution fusion | flops 202833920 | bytes 5128704 | tf_op jit(solution)/shard_map/qhc,chv->qhv/dot_general | solution.py:69
  185.3 5.0 %bitcast_reduce_fusion = (f32[16,64]{1,0:T(8,128)S(1)}, f32[8,128,64,16]{1,2,3,0:T(8,128)S(1)}) fusion(pred[8,128]{1,0:T(8,128)(4,1)S(1)} %fusion.153, bf16[256,16,576]{0,2,1:T(8,128)(2,1)} %copy-done.2, bf16[32,576,128]{2,1,0:T(8,128)(2,1)} %gather_fusion.2), kind=kOutput, calls=%fused_computation.5 | convolution fusion | flops 1211104256 | bytes 7738368 | tf_op jit(solution)/shard_map/qhc,mcp->hqmp/dot_general | solution.py:46
  190.5 1.0 fusion.7
  191.5 1.2 divide_convert_fusion
  192.7 3.9 %fusion.114 = f32[512,1024,1]{0,1,2:T(8,128)} fusion(bf16[8,128,1024]{1,2,0:T(8,128)(2,1)S(1)} %bitcast.258, bf16[32,576,128]{2,1,0:T(8,128)(2,1)} %gather_fusion.2), kind=kOutput, calls=%fused_computation.95 | convolution fusion | flops 1073741824 | bytes 5242880
  196.5 4.1 %fusion.111 = bf16[16,8,8,128]{3,2,1,0:T(8,128)(2,1)} fusion(f32[512,16,64]{0,2,1:T(8,128)} %bitcast.264, f32[16,64,64]{1,2,0:T(8,128)S(1)} %get-tuple-element.28, f32[16,64]{1,0:T(8,128)S(1)} %add.154, f32[16,64]{1,0:T(8,128)S(1)} %max.35, pred[64]{0:T(512)(128)(4,1)S(1)} %iota_compare_fusion.1, bf16[256,512]{0,1:T(8,128)(2,1)S(1)} %multiply_convert_fusion, ...), kind=kOutput, calls=%fused_computation.94 | convolution fusion | flops 202833920 | bytes 5128704 | tf_op jit(solution)/shard_map/qhc,chv->qhv/dot_general | solution.py:69
  200.8 1.1 copy_bitcast_fusion
  201.9 1.0 pad_maximum_fusion.1
  (76 shorter events, 6.1 us)
Async XLA Ops:
  6.5 38.8 %copy-start = (bf16[512,2048]{1,0:T(8,128)(2,1)S(1)}, bf16[512,2048]{1,0:T(8,128)(2,1)}, u32[]{:S(2)}) copy-start(bf16[512,2048]{1,0:T(8,128)(2,1)} %param.14) | copy-start | bytes 6291460
  18.3 11.4 %copy-start.7 = (bf16[896,576]{0,1:T(8,128)(2,1)S(1)}, bf16[896,576]{0,1:T(8,128)(2,1)}, u32[]{:S(2)}) copy-start(bf16[896,576]{0,1:T(8,128)(2,1)} %param.11) | copy-start | bytes 3096580
  18.3 120.3 %all-to-all-start = ((bf16[32,576,128]{2,1,0:T(8,128)(2,1)}), bf16[32,576,128]{2,1,0:T(8,128)(2,1)}, u32[]{:S(2)}, u32[]{:S(2)}) async-start(bf16[32,576,128]{2,1,0:T(8,128)(2,1)} %gather_fusion.1), calls=%async_computation | async-start | bytes 9437184 | tf_op jit(solution)/shard_map/all_to_all | solution.py:91
  29.7 5.0 %copy-start.11 = (s32[128]{0:T(128)S(1)}, s32[128]{0:T(128)}, u32[]{:S(2)}) copy-start(s32[128]{0:T(128)} %param.18) | copy-start | bytes 1540
  29.7 5.1 %copy-start.12 = (s32[128]{0:T(128)S(1)}, s32[128]{0:T(128)}, u32[]{:S(2)}) copy-start(s32[128]{0:T(128)} %param.19) | copy-start | bytes 1540
  29.7 71.6 %all-reduce.2.cloned.1.call-start = ((), (), s32[]{:S(2)}) async-start(), calls=%async_computation.1 | async-start | bytes 1179648 | tf_op jit(solution)/shard_map/psum | solution.py:97
  45.3 58.1 %copy-start.10 = (f32[512]{0:T(512)S(1)}, f32[512]{0:T(512)}, u32[]{:S(2)}) copy-start(f32[512]{0:T(512)} %param.12) | copy-start | bytes 6148
  107.2 3.2 %copy-start.2 = (bf16[256,16,576]{0,2,1:T(8,128)(2,1)}, bf16[256,16,576]{0,2,1:T(8,128)(2,1)S(1)}, u32[]{:S(2)}) copy-start(bf16[256,16,576]{0,2,1:T(8,128)(2,1)S(1)} %pad_maximum_fusion) | copy-start | bytes 14155780
  107.9 40.5 %copy-start.6 = (f32[16,64,64]{1,2,0:T(8,128)}, f32[16,64,64]{1,2,0:T(8,128)S(1)}, u32[]{:S(2)}) copy-start(f32[16,64,64]{1,2,0:T(8,128)S(1)} %get-tuple-element.40) | copy-start | bytes 786436
  148.5 6.2 %slice-start = ((s8[4718592]{0:T(1024)(128)(4,1)}), s8[4194304]{0:T(1024)(128)(4,1)S(1)}, s32[]{:S(2)}) async-start(s8[4718592]{0:T(1024)(128)(4,1)} %bitcast.254), calls=%async_computation.2 | async-start | bytes 8388608
  149.5 2.6 %copy-start.3 = (bf16[32,576,128]{2,1,0:T(8,128)(2,1)S(1)}, bf16[32,576,128]{2,1,0:T(8,128)(2,1)}, u32[]{:S(2)}) copy-start(bf16[32,576,128]{2,1,0:T(8,128)(2,1)} %gather_fusion.2) | copy-start | bytes 14155780
  149.6 5.1 %slice-start.1 = ((s8[4718592]{0:T(1024)(128)(4,1)}), s8[524288]{0:T(1024)(128)(4,1)S(1)}, s32[]{:S(2)}) async-start(s8[4718592]{0:T(1024)(128)(4,1)} %bitcast.254), calls=%async_computation.3 | async-start | bytes 1048576
  154.7 3.0 %copy-start.4 = (f32[16,64,64]{1,2,0:T(8,128)S(1)}, f32[16,64,64]{1,2,0:T(8,128)}, u32[]{:S(2)}) copy-start(f32[16,64,64]{1,2,0:T(8,128)} %get-tuple-element.36) | copy-start | bytes 786436
  162.7 4.1 %copy-start.5 = (f32[16,64,64]{1,2,0:T(8,128)S(1)}, f32[16,64,64]{1,2,0:T(8,128)}, u32[]{:S(2)}) copy-start(f32[16,64,64]{1,2,0:T(8,128)} %get-tuple-element.36) | copy-start | bytes 786436
  196.5 4.1 %copy-start.8 = (bf16[16,8,8,128]{3,2,1,0:T(8,128)(2,1)S(1)}, bf16[16,8,8,128]{3,2,1,0:T(8,128)(2,1)}, u32[]{:S(2)}) copy-start(bf16[16,8,8,128]{3,2,1,0:T(8,128)(2,1)} %fusion.102) | copy-start | bytes 786436
  196.5 4.1 %copy-start.9 = (bf16[16,8,8,128]{3,2,1,0:T(8,128)(2,1)S(1)}, bf16[16,8,8,128]{3,2,1,0:T(8,128)(2,1)}, u32[]{:S(2)}) copy-start(bf16[16,8,8,128]{3,2,1,0:T(8,128)(2,1)} %fusion.105) | copy-start | bytes 786436
  196.5 6.4 %copy-start.1 = (bf16[512,2048]{1,0:T(8,128)(2,1)S(1)}, bf16[512,2048]{1,0:T(8,128)(2,1)}, u32[]{:S(2)}) copy-start(bf16[512,2048]{1,0:T(8,128)(2,1)} %param.14) | copy-start | bytes 6291460
Sparse Core Ops, SparseCore 0:
  32.9 68.3 all-reduce.1
where the time goes:
time: 210 us
  waiting for transfers between devices  77.3 us (37%)
  matrix products  56.4 us (27%)
  other arithmetic  31.2 us (15%)
  local copies, waits for them, and re-layouts  19.6 us (9%)
  between operations  13.8 us (7%)
  starting transfers between devices  11.4 us (5%)
    psum x1, waiting for transfers between devices, body(): lax.psum(partial_value, 'tp')  50.2 us
    all_to_all x1, waiting for transfers between devices, body(): lax.all_to_all(store[send_slots], 'grp', split_axis=0, concat_axis=0, til...  27.1 us
    dot_general x4, matrix products, attend_local(): jnp.einsum('qhc,chv->qhv', o_lat, w_uv3, preferred_element_type=jnp.float32)  16.2 us
    dot_general x4, matrix products, attend_local(): jnp.einsum('qhc,mcp->hqmp', q_full, pages, preferred_element_type=jnp.flo...  16.1 us
    unnamed x4, matrix products  12.9 us
    all_to_all x1, starting transfers between devices, body(): lax.all_to_all(store[send_slots], 'grp', split_axis=0, concat_axis=0, til...  11.3 us
    gather x1, local copies, waits for them, and re-layouts, body(): store[send_slots]  5.66 us
    gather x1, local copies, waits for them, and re-layouts, body(): pages = arrived[placing].reshape(TR_G, MAXP, store.shape[1], store.shape[2])  5.66 us
  transfers between devices with their start and end apart: 2, of which 2 were waited for; matrix products, arithmetic and copies ran while one was open for 15% of the time, Pallas kernels for 0%

commit v1 on v0

v1 whole, which is shorter than its diff:
```python
import functools
import math

import jax
import jax.numpy as jnp
from jax import lax
from jax.experimental import pallas as pl
from jax.experimental.pallas import tpu as pltpu
from jax.sharding import PartitionSpec as P

MESH = pl.DeviceIdType.MESH
NOPE = 128
ROPE = 64
LAT = 512
VHEAD = 128
PAGE = 128
MAXP = 8
TR_G = 4
APP = 64
KVW = LAT + ROPE
HALF = KVW // 2
NEG = -1e30
NT = (((1,), (1,)), ((), ()))


def rem(a, n):
    return lax.rem(a + n, n)


def hop_order(Z):
    odd = sorted(range(1, Z, 2), key=lambda d: (min(d, Z - d), d))
    even = sorted(range(2, Z, 2), key=lambda d: (min(d, Z - d), d))
    return odd, even


def tables(pos, width):
    half = width // 2
    lane = lax.rem(lax.broadcasted_iota(jnp.int32, (1, width), 1), half)
    freq = jnp.exp(lane.astype(jnp.float32) * (-2.0 * math.log(10000.0) / width))
    angle = pos.astype(jnp.float32) * freq
    sign = jnp.where(lax.broadcasted_iota(jnp.int32, (1, width), 1) < half, -1.0, 1.0)
    return jnp.cos(angle), jnp.sin(angle) * sign


def rotate(vec, cosine, sine):
    half = vec.shape[1] // 2
    swapped = jnp.concatenate([vec[:, half:], vec[:, :half]], axis=1)
    return vec * cosine + swapped * sine


def move_kernel(
    Z, Y, X,
    pt_ref, len_ref, gain_ref, hidden_hbm, wdkv_hbm, queries_hbm, wuk_hbm, store_hbm,
    pages_hbm, q_hbm, fresh_hbm,
    store_v, staging, pages, hidden, wdkv, queries, wuk, q_v, kv_part, kv_half, kv_sib, kv_in, fresh,
    load_sem, out_sem, bar_unused, send1, recv, recv2, sendx, sendr, sends, kvsend, kvrecv,
):
    G = Z * Y
    g = lax.axis_index("grp")
    tp = lax.axis_index("tp")
    z, y = g // Y, lax.rem(g, Y)
    x, c = tp // 2, lax.rem(tp, 2)
    odd, even = hop_order(Z)
    KS = len(odd)
    KE = len(even)

    loads = [
        pltpu.make_async_copy(store_hbm, store_v, load_sem.at[0]),
        pltpu.make_async_copy(hidden_hbm, hidden, load_sem.at[1]),
        pltpu.make_async_copy(wdkv_hbm, wdkv, load_sem.at[2]),
        pltpu.make_async_copy(queries_hbm, queries, load_sem.at[3]),
        pltpu.make_async_copy(wuk_hbm, wuk, load_sem.at[4]),
    ]
    for load in loads:
        load.start()

    xr, xl, xo = rem(x + 1, X), rem(x - 1, X), rem(x + 2, X)
    dev_r, dev_l, dev_o, dev_s = (
        (g, xr * 2 + c), (g, xl * 2 + c), (g, xo * 2 + c), (g, x * 2 + 1 - c)
    )

    def hop(k):
        return jnp.where(c == 1, odd[k], even[k] if k < KE else odd[k])

    def to_group(dz, dy):
        return rem(z + dz, Z) * Y + rem(y + dy, Y)

    def dy_of(dz):
        return lax.rem(dz + x, Y)

    def both(k, fn):
        if k < KE:
            fn()
        else:
            pl.when(c == 1)(fn)

    def direct(d, fn):
        pl.when(c == (1 if d == Y - 1 else 0))(fn)

    barrier = pltpu.get_barrier_semaphore()

    def greet(dev):
        pl.semaphore_signal(barrier, inc=1, device_id=dev, device_id_type=MESH)

    for dev in (dev_r, dev_l, dev_o, dev_s):
        greet(dev)
    for k in range(KS):
        both(k, lambda: greet((to_group(-hop(k), -dy_of(hop(k))), tp)))
    for d in range(1, Y):
        direct(d, lambda: greet((to_group(0, -d), tp)))

    def find(dest):
        found = jnp.int32(0)
        for t in range(TR_G):
            for m in range(MAXP):
                value = pt_ref[dest * TR_G + t, m]
                found = found + jnp.where(value // G == g, lax.rem(value, G), 0)
        return found

    picks = []
    for k in range(KS):
        picks.append(find(to_group(hop(k), dy_of(hop(k)))))
    mine = find(g)
    d_one = jnp.where(c == 1, Y - 1, 1)
    pick_one = find(to_group(0, d_one))
    pick_two = find(to_group(0, 2))

    loads[0].wait()
    for k in range(KS):
        staging[k] = store_v[picks[k]]
    staging[KS] = store_v[pick_one]
    staging[KS + 1] = store_v[pick_two]
    pages[0] = store_v[mine]

    pl.semaphore_wait(barrier, KS + 5)

    def rcopy(src, dst, ss, rs, dev):
        return pltpu.make_async_remote_copy(
            src_ref=src, dst_ref=dst, send_sem=ss, recv_sem=rs, device_id=dev, device_id_type=MESH
        )

    def first(k):
        dz = hop(k)
        slot = dz * Y + x
        return rcopy(staging.at[k], pages.at[slot], send1.at[k], recv.at[slot], (to_group(dz, dy_of(dz)), tp))

    def first_direct(d):
        at = KS + (1 if d == 2 else 0)
        return rcopy(staging.at[at], pages.at[d], send1.at[at], recv.at[d], (to_group(0, d), tp))

    for k in range(KS):
        both(k, lambda: first(k).start())
    for d in range(1, Y):
        direct(d, lambda: first_direct(d).start())

    loads[1].wait()
    loads[2].wait()
    rows = hidden.shape[0]
    hrows = rows // 2
    brows = hrows // X
    kv_part[...] = jnp.dot(hidden[...], wdkv[...], preferred_element_type=jnp.float32)
    sib_kv = rcopy(kv_part.at[pl.ds((1 - c) * hrows, hrows)], kv_sib, kvsend.at[0], kvrecv.at[0], dev_s)
    sib_kv.start()

    tok = lax.broadcasted_iota(jnp.int32, (APP, 1), 0)
    pos = jnp.concatenate([tok + len_ref[g * TR_G + t] for t in range(TR_G)], axis=0)
    cosine, sine = tables(pos, ROPE)

    sib_kv.wait()
    kv_half[...] = kv_part[pl.ds(c * hrows, hrows), :] + kv_sib[...]
    kv_x = []
    for n, (xx, dev) in enumerate(((xr, dev_r), (xl, dev_l), (xo, dev_o))):
        copy = rcopy(kv_half.at[pl.ds(xx * brows, brows)], kv_in.at[n], kvsend.at[1 + n], kvrecv.at[1 + n], dev)
        copy.start()
        kv_x.append(copy)

    loads[3].wait()
    loads[4].wait()
    heads = wuk.shape[1] // NOPE
    blocks = rows // 16

    def q_head(h):
        base = h * (NOPE + ROPE)
        nope = queries[:, base : base + NOPE]
        lat = lax.dot_general(
            nope, wuk[:, h * NOPE : (h + 1) * NOPE], NT, preferred_element_type=jnp.float32
        ).astype(jnp.bfloat16)
        rot = rotate(queries[:, base + NOPE : base + NOPE + ROPE].astype(jnp.float32), cosine, sine)
        q_v[:, h * 16 : (h + 1) * 16, 0:LAT] = lat.reshape(blocks, 16, LAT)
        q_v[:, h * 16 : (h + 1) * 16, LAT:KVW] = rot.astype(jnp.bfloat16).reshape(blocks, 16, ROPE)

    for h in range(heads // 2):
        q_head(h)

    for copy in kv_x:
        copy.wait()
    kv = kv_half[pl.ds(x * brows, brows), :] + kv_in[0] + kv_in[1] + kv_in[2]
    lat = kv[:, :LAT]
    factor = lax.rsqrt(jnp.mean(lat * lat, axis=-1, keepdims=True) + 1e-06)
    lat = lat * factor * gain_ref[...]
    row0 = c * hrows + x * brows
    mypos = len_ref[g * TR_G + row0 // APP] + lax.rem(row0, APP)
    mycos, mysin = tables(mypos + lax.broadcasted_iota(jnp.int32, (brows, 1), 0), ROPE)
    myrope = rotate(kv[:, LAT:], mycos, mysin)
    fresh[pl.ds(row0, brows), 0:LAT] = lat.astype(jnp.bfloat16)
    fresh[pl.ds(row0, brows), LAT:KVW] = myrope.astype(jnp.bfloat16)
    fr_x = []
    for n, dev in enumerate((dev_r, dev_l, dev_o)):
        part = fresh.at[pl.ds(row0, brows)]
        copy = rcopy(part, part, kvsend.at[4 + n], kvrecv.at[4 + n], dev)
        copy.start()
        fr_x.append(copy)

    for h in range(heads // 2, heads):
        q_head(h)
    q_out = pltpu.make_async_copy(q_v, q_hbm, out_sem.at[0])
    q_out.start()

    def to_sib(slot, n):
        return rcopy(pages.at[slot], pages.at[slot], sends.at[n], recv.at[slot], dev_s)

    def to_x(slot, k, n, dev):
        return rcopy(pages.at[slot], pages.at[slot], sendx.at[k, n], recv.at[slot], dev)

    def relay(slot, k, n, dev):
        part = pages.at[slot, pl.ds(n * HALF, HALF)]
        return rcopy(part, part, sendr.at[k, n], (recv2 if n else recv).at[slot], dev)

    def slots_of(k):
        dz = hop(k) * Y
        return dz + x, dz + xl, dz + xr, dz + xo

    def own_step(k):
        own = slots_of(k)[0]
        first(k).wait_recv()
        to_x(own, k, 0, dev_r).start()
        to_x(own, k, 1, dev_l).start()
        to_sib(own, 4 * k).start()

    def side_step(k):
        _, left, right, _ = slots_of(k)
        to_x(left, k, 0, dev_r).wait_recv()
        relay(left, k, 0, dev_r).start()
        to_sib(left, 4 * k + 1).start()
        to_x(right, k, 1, dev_l).wait_recv()
        relay(right, k, 1, dev_l).start()
        to_sib(right, 4 * k + 2).start()

    def far_step(k):
        far = slots_of(k)[3]
        relay(far, k, 0, dev_r).wait_recv()
        relay(far, k, 1, dev_l).wait_recv()
        to_sib(far, 4 * k + 3).start()

    def direct_step(d):
        first_direct(d).wait_recv()
        to_sib(d, 4 * KS + (1 if d == 2 else 0)).start()

    for d in range(1, Y):
        direct(d, lambda: direct_step(d))
    for step in range(KS + 2):
        if step < KS:
            both(step, lambda: own_step(step))
        if 0 <= step - 1 < KS:
            both(step - 1, lambda: side_step(step - 1))
        if 0 <= step - 2 < KS:
            both(step - 2, lambda: far_step(step - 2))

    for copy in fr_x:
        copy.wait()
    part = fresh.at[pl.ds(c * hrows, hrows)]
    fr_s = rcopy(part, part, kvsend.at[7], kvrecv.at[7], dev_s)
    fr_s.start()

    for k in range(KS):
        other = jnp.where(c == 0, odd[k], even[k] if k < KE else odd[k]) * Y

        def take():
            for n in range(X):
                to_sib(other + n, 0).wait_recv()

        if k < KE:
            take()
        else:
            pl.when(c == 0)(take)
    for d in range(1, Y):
        pl.when(c != (1 if d == Y - 1 else 0))(lambda: to_sib(d, 0).wait_recv())
    fr_s.wait()
    f_out = pltpu.make_async_copy(fresh, fresh_hbm, out_sem.at[1])
    f_out.start()
    p_out = pltpu.make_async_copy(pages, pages_hbm, out_sem.at[2])
    p_out.start()

    def drain(k):
        first(k).wait_send()
        own, left, right, far = slots_of(k)
        to_x(own, k, 0, dev_r).wait_send()
        to_x(own, k, 1, dev_l).wait_send()
        relay(left, k, 0, dev_r).wait_send()
        relay(right, k, 1, dev_l).wait_send()
        for n, slot in enumerate((own, left, right, far)):
            to_sib(slot, 4 * k + n).wait_send()

    def drain_direct(d):
        first_direct(d).wait_send()
        to_sib(d, 4 * KS + (1 if d == 2 else 0)).wait_send()

    for k in range(KS):
        both(k, lambda: drain(k))
    for d in range(1, Y):
        direct(d, lambda: drain_direct(d))
    q_out.wait()
    f_out.wait()
    p_out.wait()


def attend_kernel(
    Z, Y,
    pt_ref, len_ref, app_ref, pages_hbm, q_hbm, fresh_hbm, wuv_hbm,
    out_ref,
    kt, q_v, fresh, wuv, s_ref, p_ref, o_ref,
    page_sem, q_sem, sem,
):
    G = Z * Y
    g = lax.axis_index("grp")
    z, y = g // Y, lax.rem(g, Y)
    f_in = pltpu.make_async_copy(fresh_hbm, fresh, sem.at[0])
    f_in.start()
    blocks = APP // 16
    q_in, page_in = [], []
    for t in range(TR_G):
        copy = pltpu.make_async_copy(
            q_hbm.at[pl.ds(t * blocks, blocks)], q_v.at[pl.ds(t * blocks, blocks)], q_sem.at[t]
        )
        copy.start()
        q_in.append(copy)
        for m in range(MAXP):
            source = pt_ref[g * TR_G + t, m] // G
            dz = rem(z - source // Y, Z)
            dy = rem(y - lax.rem(source, Y), Y)
            slot = jnp.where(dz == 0, dy, dz * Y + lax.rem(dy - dz + 2 * Z * Y, Y))
            copy = pltpu.make_async_copy(
                pages_hbm.at[slot], kt.at[t, :, pl.ds(m * PAGE, PAGE)], page_sem.at[t, m]
            )
            copy.start()
            page_in.append(copy)
    w_in = pltpu.make_async_copy(wuv_hbm, wuv, sem.at[1])
    w_in.start()
    f_in.wait()
    scale = math.log2(math.e) / math.sqrt(NOPE + ROPE)
    WIDE = 256
    heads = wuv.shape[1] // VHEAD
    for t in range(TR_G):
        q_in[t].wait()
        for m in range(MAXP):
            page_in[t * MAXP + m].wait()
        length = len_ref[g * TR_G + t]
        count = app_ref[g * TR_G + t]

        def block(jb, _):
            q = q_v[t * blocks + jb]
            top = None
            for n in range(MAXP * PAGE // WIDE):
                s = jnp.dot(q, kt[t, :, n * WIDE : (n + 1) * WIDE], preferred_element_type=jnp.float32) * scale
                if (n + 1) * WIDE > MAXP * PAGE // 2:
                    spot = n * WIDE + lax.broadcasted_iota(jnp.int32, (1, WIDE), 1)
                    s = s + jnp.where(spot < length, 0.0, NEG)
                s_ref[:, n * WIDE : (n + 1) * WIDE] = s
                part = jnp.maximum(s[:, :128], s[:, 128:])
                top = part if top is None else jnp.maximum(top, part)
            fr = fresh[t * APP : (t + 1) * APP, :]
            s = lax.dot_general(q, fr, NT, preferred_element_type=jnp.float32) * scale
            row = lax.broadcasted_iota(jnp.int32, (q.shape[0], APP), 0)
            col = lax.broadcasted_iota(jnp.int32, (q.shape[0], APP), 1)
            s = jnp.where((col <= jb * 16 + lax.rem(row, 16)) & (col < count), s, NEG)
            top = jnp.maximum(jnp.max(top, axis=1, keepdims=True), jnp.max(s, axis=1, keepdims=True))
            p = jnp.exp2(s - top)
            total = jnp.sum(p, axis=1, keepdims=True)
            acc = jnp.dot(p.astype(jnp.bfloat16), fr[:, :LAT], preferred_element_type=jnp.float32)
            sums = None
            for n in range(MAXP * PAGE // WIDE):
                p = jnp.exp2(s_ref[:, n * WIDE : (n + 1) * WIDE] - top)
                part = p[:, :128] + p[:, 128:]
                sums = part if sums is None else sums + part
                p_ref[:, n * WIDE : (n + 1) * WIDE] = p.astype(jnp.bfloat16)
            total = total + jnp.sum(sums, axis=1, keepdims=True)
            acc = acc + lax.dot_general(p_ref[...], kt[t, 0:LAT, :], NT, preferred_element_type=jnp.float32)
            o = (acc * (1.0 / total)).astype(jnp.bfloat16)
            o_ref[:, pl.ds(pl.multiple_of(t * APP + jb * 16, 16), 16), :] = o.reshape(heads, 16, LAT)
            return 0

        lax.fori_loop(0, (count + 15) // 16, block, 0)
    w_in.wait()
    tok = lax.broadcasted_iota(jnp.int32, (APP, 1), 0)
    valid = jnp.concatenate([tok < app_ref[g * TR_G + t] for t in range(TR_G)], axis=0)
    for h in range(heads):
        out = jnp.dot(o_ref[h], wuv[:, h * VHEAD : (h + 1) * VHEAD], preferred_element_type=jnp.float32)
        out_ref[:, h * VHEAD : (h + 1) * VHEAD] = jnp.where(valid, out, 0.0).astype(jnp.bfloat16)


def body(Z, Y, X, hidden, w_dkv, kv_gain, queries, w_uk, w_uv, store, page_table, cached_len, app_len):
    bf, f32 = jnp.bfloat16, jnp.float32
    rows = hidden.shape[0]
    heads = w_uk.shape[1] // NOPE
    G = Z * Y
    KS = len(hop_order(Z)[0])
    any_spec = pl.BlockSpec(memory_space=pl.ANY)
    smem = pl.BlockSpec(memory_space=pltpu.SMEM)
    vmem = pl.BlockSpec(memory_space=pltpu.VMEM)
    blocks, brow = rows // 16, heads * 16
    hrows = rows // 2
    pages, q_full, fresh = pl.pallas_call(
        functools.partial(move_kernel, Z, Y, X),
        out_shape=(
            jax.ShapeDtypeStruct((G, KVW, PAGE), bf),
            jax.ShapeDtypeStruct((blocks, brow, KVW), bf),
            jax.ShapeDtypeStruct((rows, KVW), bf),
        ),
        in_specs=[smem, smem, vmem] + [any_spec] * 5,
        out_specs=(any_spec,) * 3,
        scratch_shapes=[
            pltpu.VMEM((G, KVW, PAGE), bf),
            pltpu.VMEM((KS + 2, KVW, PAGE), bf),
            pltpu.VMEM((G, KVW, PAGE), bf),
            pltpu.VMEM(hidden.shape, bf),
            pltpu.VMEM(w_dkv.shape, bf),
            pltpu.VMEM(queries.shape, bf),
            pltpu.VMEM(w_uk.shape, bf),
            pltpu.VMEM((blocks, brow, KVW), bf),
            pltpu.VMEM((rows, KVW), f32),
            pltpu.VMEM((hrows, KVW), f32),
            pltpu.VMEM((hrows, KVW), f32),
            pltpu.VMEM((3, hrows // X, KVW), f32),
            pltpu.VMEM((rows, KVW), bf),
            pltpu.SemaphoreType.DMA((5,)),
            pltpu.SemaphoreType.DMA((3,)),
            pltpu.SemaphoreType.DMA((1,)),
            pltpu.SemaphoreType.DMA((KS + 2,)),
            pltpu.SemaphoreType.DMA((G,)),
            pltpu.SemaphoreType.DMA((G,)),
            pltpu.SemaphoreType.DMA((KS, 2)),
            pltpu.SemaphoreType.DMA((KS, 2)),
            pltpu.SemaphoreType.DMA((4 * KS + 2,)),
            pltpu.SemaphoreType.DMA((8,)),
            pltpu.SemaphoreType.DMA((8,)),
        ],
        compiler_params=pltpu.CompilerParams(
            collective_id=0, has_side_effects=True, vmem_limit_bytes=56 * 1024 * 1024
        ),
        name="move",
    )(page_table, cached_len, kv_gain[None, :], hidden, w_dkv, queries, w_uk, store)
    return pl.pallas_call(
        functools.partial(attend_kernel, Z, Y),
        out_shape=jax.ShapeDtypeStruct((rows, heads * VHEAD), bf),
        in_specs=[smem, smem, smem] + [any_spec] * 4,
        out_specs=vmem,
        scratch_shapes=[
            pltpu.VMEM((TR_G, KVW, MAXP * PAGE), bf),
            pltpu.VMEM((blocks, brow, KVW), bf),
            pltpu.VMEM((rows, KVW), bf),
            pltpu.VMEM(w_uv.shape, bf),
            pltpu.VMEM((brow, MAXP * PAGE), f32),
            pltpu.VMEM((brow, MAXP * PAGE), bf),
            pltpu.VMEM((heads, rows, LAT), bf),
            pltpu.SemaphoreType.DMA((TR_G, MAXP)),
            pltpu.SemaphoreType.DMA((TR_G,)),
            pltpu.SemaphoreType.DMA((2,)),
        ],
        compiler_params=pltpu.CompilerParams(vmem_limit_bytes=56 * 1024 * 1024),
        name="attend",
    )(page_table, cached_len, app_len, pages, q_full, fresh, w_uv)


def solution(mesh):
    X = mesh.shape["tp"] // 2
    Y = X
    Z = mesh.shape["grp"] // Y
    in_specs = (
        P("grp", "tp"),
        P("tp", None),
        P(),
        P("grp", "tp"),
        P(None, "tp"),
        P(None, "tp"),
        P("grp", None, None),
        P(),
        P(),
        P(),
    )
    return jax.shard_map(
        functools.partial(body, Z, Y, X), mesh=mesh, in_specs=in_specs, out_specs=P("grp", "tp"), check_vma=False
    )
```

time: 210 us -> 75 us (0.36)
  the two profiles are of different devices: /device:TPU:15 before, /device:TPU:27 now
where the time goes in v1:
time: 75 us; the launch traced here: 74.7 us
  Pallas kernels  70.9 us (95%)
  local copies, waits for them, and re-layouts  3.78 us (5%)
    pallas_call x1, Pallas kernels, body(): pl.pallas_call(functools.partial(move_kernel, Z, Y, X), out_shape=(jax.Sh...  45.6 us
    pallas_call x1, Pallas kernels, body(): pl.pallas_call(functools.partial(attend_kernel, Z, Y), out_shape=jax.Shap...  25.2 us
    unnamed x2, local copies, waits for them, and re-layouts  3.78 us

profile of v1, /device:TPU:27, one launch (start us, length us, event | category | flops | bytes accessed | tf_op | source)
XLA Modules:
  0.0 74.7 jit_solution(13035816668594912627)
XLA Ops:
  0.0 1.4 %copy.13.pt_ref = s32[128,8]{1,0:T(8,128)} copy(s32[128,8]{0,1:T(8,128)} %param.17) | data formatting | bytes 8192 | tf_op args[7]
  1.4 2.4 %copy.12.wdkv_hbm = bf16[896,576]{1,0:T(8,128)(2,1)} copy(bf16[896,576]{0,1:T(8,128)(2,1)} %param.11) | data formatting | bytes 2064384 | tf_op args[1]
  3.8 45.6 %move.1 = (bf16[32,576,128]{2,1,0:T(8,128)(2,1)}, bf16[16,256,576]{2,1,0:T(8,128)(2,1)}, bf16[256,576]{1,0:T(8,128)(2,1)}) custom-call(s32[128,8]{1,0:T(8,128)} %copy.13.pt_ref, s32[128]{0:T(128)} %len_ref.3, f32[1,512]{1,0:T(1,128)} %bitcast.1, bf16[256,896]{1,0:T(8,128)(2,1)} %hidden_hbm.1, bf16[896,576]{1,0:T(8,128)(2,1)} %copy.12.wdkv_hbm, ...), custom_call_target="tpu_custom_call" | custom-call | tf_op jit(solution)/shard_map/move/pallas_call | solution.py:412
  49.4 25.2 %attend.1 = bf16[256,2048]{1,0:T(8,128)(2,1)} custom-call(s32[128,8]{1,0:T(8,128)} %copy.13.pt_ref, s32[128]{0:T(128)} %len_ref.3, s32[128]{0:T(128)} %app_ref.1, bf16[32,576,128]{2,1,0:T(8,128)(2,1)} %get-tuple-element.8.pages_hbm, bf16[16,256,576]{2,1,0:T(8,128)(2,1)} %get-tuple-element.9.q_hbm, bf16[256,576]{1,0:T(8,128)(2,1)} %get-tuple-element.10.fresh_hbm, ...), custom_call_target="tpu_custom_call" | custom-call | tf_op jit(solution)/shard_map/attend/pallas_call | solution.py:452

commit v2 on v0

v2 whole, which is shorter than its diff:
```python
import functools
import math

import jax
import jax.numpy as jnp
from jax import lax
from jax.experimental import pallas as pl
from jax.experimental.pallas import tpu as pltpu
from jax.sharding import PartitionSpec as P

MESH = pl.DeviceIdType.MESH
NOPE = 128
ROPE = 64
LAT = 512
VHEAD = 128
PAGE = 128
MAXP = 8
TR_G = 4
APP = 64
KVW = LAT + ROPE
NEG = -1e30
NT = (((1,), (1,)), ((), ()))
PHASES = (32, 32, 32, 32)
CHUNK = 128
SCALE = math.log2(math.e) / math.sqrt(NOPE + ROPE)
bf16, f32 = jnp.bfloat16, jnp.float32


def rem(a, n):
    return lax.rem(a + n, n)


def tables(pos, width):
    half = width // 2
    lane = lax.rem(lax.broadcasted_iota(jnp.int32, (1, width), 1), half)
    freq = jnp.exp(lane.astype(f32) * (-2.0 * math.log(10000.0) / width))
    angle = pos.astype(f32) * freq
    sign = jnp.where(lax.broadcasted_iota(jnp.int32, (1, width), 1) < half, -1.0, 1.0)
    return jnp.cos(angle), jnp.sin(angle) * sign


def rotate(vec, cosine, sine):
    half = vec.shape[1] // 2
    swapped = jnp.concatenate([vec[:, half:], vec[:, :half]], axis=1)
    return vec * cosine + swapped * sine


def kernel(
    Z, Y, X,
    pt_ref, len_ref, app_ref, gain_ref, hidden_hbm, wdkv_hbm, queries_hbm, wuk_hbm, wuv_hbm, store_hbm,
    out_hbm,
    *scratch,
):
    n_ph = len(PHASES)
    (store_v, hidden, wdkv, queries, wuk, wuv, q_v, kv_part, kv_half, kv_sib, kv_in, fresh,
     m_ref, l_ref, acc_ref, s_a, s_b, p_ref, kt_a, kt_b, o_ref, out_v,
     load_sem, out_sem, send1, recv1, sendx, recvx, sendr, recvr, sends, recvs, kvsend, kvrecv) = scratch[: -2 * n_ph]
    stage = scratch[-2 * n_ph : -n_ph]
    pages = scratch[-n_ph:]
    s_refs, kts = (s_a, s_b), (kt_a, kt_b)
    G = Z * Y
    KC = Z // 2
    g = lax.axis_index("grp")
    tp = lax.axis_index("tp")
    z, y = g // Y, lax.rem(g, Y)
    x, c = tp // 2, lax.rem(tp, 2)
    heads = wuk.shape[1] // NOPE
    rows = hidden.shape[0]
    starts = [sum(PHASES[:i]) for i in range(n_ph)]

    loads = [
        pltpu.make_async_copy(src, dst, load_sem.at[i])
        for i, (src, dst) in enumerate(
            ((store_hbm, store_v), (hidden_hbm, hidden), (wdkv_hbm, wdkv), (queries_hbm, queries),
             (wuk_hbm, wuk), (wuv_hbm, wuv))
        )
    ]
    for load in loads:
        load.start()

    xr, xl, xo = rem(x + 1, X), rem(x - 1, X), rem(x + 2, X)
    dev_r, dev_l, dev_o, dev_s = (
        (g, xr * 2 + c), (g, xl * 2 + c), (g, xo * 2 + c), (g, x * 2 + 1 - c)
    )
    is_self = (x == 0) & (c == 0)

    def remote(k, fn):
        if k == 0:
            pl.when(jnp.logical_not(is_self))(fn)
        else:
            fn()

    def group(k, way):
        dz = 2 * k + c
        dy = lax.rem(dz + x, Y)
        return rem(z + way * dz, Z) * Y + rem(y + way * dy, Y)

    barrier = pltpu.get_barrier_semaphore()

    def greet(dev):
        pl.semaphore_signal(barrier, inc=1, device_id=dev, device_id_type=MESH)

    for dev in (dev_r, dev_l, dev_o, dev_s):
        greet(dev)
    for k in range(KC):
        remote(k, lambda: greet((group(k, -1), tp)))

    def find(dest):
        found = jnp.int32(0)
        for t in range(TR_G):
            for m in range(MAXP):
                value = pt_ref[m, dest * TR_G + t]
                found = found + jnp.where(value // G == g, lax.rem(value, G), 0)
        return found

    picks = [find(group(k, 1)) for k in range(KC)]

    def rcopy(src, dst, ss, rs, dev):
        return pltpu.make_async_remote_copy(
            src_ref=src, dst_ref=dst, send_sem=ss, recv_sem=rs, device_id=dev, device_id_type=MESH
        )

    def slot(who):
        return c * (X * KC) + who * KC

    def first(q, k):
        return rcopy(stage[q].at[k], pages[q].at[slot(x) + k], send1.at[q, k], recv1.at[q, k], (group(k, 1), tp))

    loads[0].wait()
    for k in range(KC):
        page = store_v[picks[k]]
        lat, rope = page[0:LAT, :].T, page[LAT:KVW, :].T
        for q in range(n_ph):
            stage[q][k, :, 0:LAT] = lat[starts[q] : starts[q] + PHASES[q], :]
            stage[q][k, :, LAT:KVW] = rope[starts[q] : starts[q] + PHASES[q], :]

    @pl.when(is_self)
    def _():
        for q in range(n_ph):
            pages[q][0] = stage[q][0]

    pl.semaphore_wait(barrier, KC + 4 - is_self.astype(jnp.int32))
    for q in range(n_ph):
        for k in reversed(range(KC)):
            remote(k, lambda: first(q, k).start())

    def to_x(q, who, n, dev):
        part = pages[q].at[pl.ds(slot(who), KC)]
        return rcopy(part, part, sendx.at[q, n], recvx.at[q, n], dev)

    def relay(q, who, n, dev):
        part = pages[q].at[pl.ds(slot(who) + n * (KC // 2), KC // 2)]
        return rcopy(part, part, sendr.at[q, n], recvr.at[q, n], dev)

    def to_sib(q, n):
        part = pages[q].at[pl.ds(slot((x, xl, xr, xo)[n]), KC)]
        return rcopy(part, part, sends.at[q, n], recvs.at[q, n], dev_s)

    def from_sib(q, n):
        part = pages[q].at[pl.ds((1 - c) * (X * KC) + (x, xl, xr, xo)[n] * KC, KC)]
        return rcopy(part, part, sends.at[q, n], recvs.at[q, n], dev_s)

    def step_own(q):
        for k in range(KC):
            remote(k, lambda: first(q, k).wait_recv())
        to_x(q, x, 0, dev_r).start()
        to_x(q, x, 1, dev_l).start()
        to_sib(q, 0).start()

    def step_side(q):
        to_x(q, xl, 0, dev_r).wait_recv()
        relay(q, xl, 0, dev_r).start()
        to_sib(q, 1).start()
        to_x(q, xr, 1, dev_l).wait_recv()
        relay(q, xr, 1, dev_l).start()
        to_sib(q, 2).start()

    def step_far(q):
        relay(q, xo, 0, dev_r).wait_recv()
        relay(q, xo, 1, dev_l).wait_recv()
        to_sib(q, 3).start()

    def step_done(q):
        for n in range(4):
            from_sib(q, n).wait_recv()

    hrows = rows // 2
    brows = hrows // X
    row0 = c * hrows + x * brows

    sib_kv = rcopy(kv_part.at[pl.ds((1 - c) * hrows, hrows)], kv_sib, kvsend.at[0], kvrecv.at[0], dev_s)
    kv_x = [
        rcopy(kv_half.at[pl.ds(xx * brows, brows)], kv_in.at[n], kvsend.at[1 + n], kvrecv.at[1 + n], dev)
        for n, (xx, dev) in enumerate(((xr, dev_r), (xl, dev_l), (xo, dev_o)))
    ]
    block = fresh.at[pl.ds(row0, brows)]
    fr_x = [
        rcopy(block, block, kvsend.at[4 + n], kvrecv.at[4 + n], dev)
        for n, dev in enumerate((dev_r, dev_l, dev_o))
    ]
    half = fresh.at[pl.ds(c * hrows, hrows)]
    fr_s = rcopy(half, half, kvsend.at[7], kvrecv.at[7], dev_s)

    def kv_one():
        loads[1].wait()
        loads[2].wait()
        kv_part[...] = lax.dot_general(hidden[...], wdkv[...], NT, preferred_element_type=f32)
        sib_kv.start()

    def kv_two():
        sib_kv.wait()
        kv_half[...] = kv_part[pl.ds(c * hrows, hrows), :] + kv_sib[...]
        for copy in kv_x:
            copy.start()

    def kv_three():
        for copy in kv_x:
            copy.wait()
        kv = kv_half[pl.ds(x * brows, brows), :] + kv_in[0] + kv_in[1] + kv_in[2]
        lat = kv[:, :LAT]
        factor = lax.rsqrt(jnp.mean(lat * lat, axis=-1, keepdims=True) + 1e-06)
        lat = lat * factor * gain_ref[...]
        mypos = len_ref[g * TR_G + row0 // APP] + lax.rem(row0, APP)
        mycos, mysin = tables(mypos + lax.broadcasted_iota(jnp.int32, (brows, 1), 0), ROPE)
        fresh[pl.ds(row0, brows), 0:LAT] = lat.astype(bf16)
        fresh[pl.ds(row0, brows), LAT:KVW] = rotate(kv[:, LAT:], mycos, mysin).astype(bf16)
        for copy in fr_x:
            copy.start()

    def kv_four():
        for copy in fr_x:
            copy.wait()
        fr_s.start()

    def q_heads(first_head, last_head, angles):
        cosine, sine = angles
        for h in range(first_head, last_head):
            base = h * (NOPE + ROPE)
            lat = lax.dot_general(
                queries[:, base : base + NOPE], wuk[:, h * NOPE : (h + 1) * NOPE], NT, preferred_element_type=f32
            ).astype(bf16)
            rot = rotate(queries[:, base + NOPE : base + NOPE + ROPE].astype(f32), cosine, sine).astype(bf16)
            at = slice(h * APP, (h + 1) * APP)
            q_v[:, at, 0:LAT] = lat.reshape(TR_G, APP, LAT)
            q_v[:, at, LAT:KVW] = rot.reshape(TR_G, APP, ROPE)

    def start_softmax(t):
        count = app_ref[g * TR_G + t]
        fr = fresh[t * APP : (t + 1) * APP, :]
        s_refs[0][:, 0:APP] = lax.dot_general(q_v[t], fr, NT, preferred_element_type=f32)
        col = lax.broadcasted_iota(jnp.int32, (CHUNK, APP), 1)
        row = lax.rem(lax.broadcasted_iota(jnp.int32, (CHUNK, APP), 0), APP)
        allowed = (col <= row) & (col < count)
        for r in range(0, heads * APP, CHUNK):
            s = jnp.where(allowed, s_refs[0][r : r + CHUNK, 0:APP] * SCALE, NEG)
            top = jnp.max(s, axis=1, keepdims=True)
            p = jnp.exp2(s - top)
            m_ref[t, r : r + CHUNK, :] = jnp.broadcast_to(top, (CHUNK, 128))
            l_ref[t, r : r + CHUNK, :] = jnp.concatenate([p, jnp.zeros((CHUNK, 128 - APP), f32)], axis=1)
            p_ref[r : r + CHUNK, 0:APP] = p.astype(bf16)
        acc_ref[t] = jnp.dot(p_ref[:, 0:APP], fr[:, 0:LAT], preferred_element_type=f32)

    def scores(q, t, b):
        width = PHASES[q]
        for m in range(MAXP):
            source = pt_ref[m, g * TR_G + t] // G
            dz = rem(z - source // Y, Z)
            dy = rem(y - lax.rem(source, Y), Y)
            at = lax.rem(dz, 2) * (X * KC) + lax.rem(dy - dz + 2 * Z * Y, Y) * KC + dz // 2
            kts[b][m * width : (m + 1) * width, :] = pages[q][at]
        n = MAXP * width
        s_refs[b][:, 0:n] = lax.dot_general(q_v[t], kts[b][0:n, :], NT, preferred_element_type=f32)

    def combine(q, t, b):
        width = PHASES[q]
        n = MAXP * width
        col = lax.broadcasted_iota(jnp.int32, (1, n), 1)
        spot = col // width * PAGE + starts[q] + lax.rem(col, width)
        bias = jnp.where(spot < len_ref[g * TR_G + t], 0.0, NEG)
        for r in range(0, heads * APP, CHUNK):
            at = slice(r, r + CHUNK)
            s = s_refs[b][at, 0:n] * SCALE + bias
            old = m_ref[t, at, :]
            top = jnp.maximum(old, jnp.max(s, axis=1, keepdims=True))
            keep = jnp.exp2(old - top)
            m_ref[t, at, :] = top
            total = l_ref[t, at, :] * keep
            for j in range(0, n, 128):
                p = jnp.exp2(s[:, j : j + 128] - top)
                total = total + p
                p_ref[at, j : j + 128] = p.astype(bf16)
            l_ref[t, at, :] = total
            for j in range(0, LAT, 128):
                acc_ref[t, at, j : j + 128] = acc_ref[t, at, j : j + 128] * keep
        acc_ref[t] = acc_ref[t] + jnp.dot(p_ref[:, 0:n], kts[b][0:n, 0:LAT], preferred_element_type=f32)

    def finish(t):
        for r in range(0, heads * APP, CHUNK):
            total = jnp.sum(l_ref[t, r : r + CHUNK, :], axis=1, keepdims=True)
            o = (acc_ref[t, r : r + CHUNK, :] * (1.0 / total)).astype(bf16)
            o_ref[r // APP : (r + CHUNK) // APP, t * APP : (t + 1) * APP, :] = o.reshape(CHUNK // APP, APP, LAT)

    kv_one()
    tok = lax.broadcasted_iota(jnp.int32, (APP, 1), 0)
    pos = jnp.concatenate([tok + len_ref[g * TR_G + t] for t in range(TR_G)], axis=0)
    angles = tables(pos, ROPE)
    kv_two()
    loads[3].wait()
    loads[4].wait()
    q_heads(0, heads // 2, angles)
    step_own(0)
    kv_three()
    q_heads(heads // 2, heads, angles)
    step_own(1)
    kv_four()
    step_side(0)
    step_own(2)
    fr_s.wait()
    start_softmax(0)
    start_softmax(1)
    step_far(0)
    step_side(1)
    start_softmax(2)
    start_softmax(3)
    step_own(3)

    before = {
        (0, 0): [(step_done, 0)],
        (0, 2): [(step_far, 1), (step_side, 2)],
        (1, 0): [(step_done, 1)],
        (1, 1): [(step_far, 2)],
        (1, 2): [(step_side, 3)],
        (2, 0): [(step_done, 2)],
        (2, 2): [(step_far, 3)],
        (3, 0): [(step_done, 3)],
    }
    units = [(q, t) for q in range(n_ph) for t in range(TR_G)]
    for i, (q, t) in enumerate(units):
        for step, arg in before.get((q, t), ()):
            step(arg)
        scores(q, t, i % 2)
        if i > 0:
            pq, pt = units[i - 1]
            combine(pq, pt, (i - 1) % 2)
            if pq == n_ph - 1:
                finish(pt)
    combine(*units[-1], (len(units) - 1) % 2)
    finish(TR_G - 1)

    loads[5].wait()
    valid = jnp.concatenate([tok < app_ref[g * TR_G + t] for t in range(TR_G)], axis=0)
    outs = []
    for part in range(4):
        for h in range(part * heads // 4, (part + 1) * heads // 4):
            o = jnp.dot(o_ref[h], wuv[:, h * VHEAD : (h + 1) * VHEAD], preferred_element_type=f32)
            out_v[:, h * VHEAD : (h + 1) * VHEAD] = jnp.where(valid, o, 0.0).astype(bf16)
        wide = heads * VHEAD // 4
        at = pl.ds(part * wide, wide)
        copy = pltpu.make_async_copy(out_v.at[:, at], out_hbm.at[:, at], out_sem.at[part])
        copy.start()
        outs.append(copy)

    for q in range(n_ph):
        for k in range(KC):
            remote(k, lambda: first(q, k).wait_send())
        to_x(q, x, 0, dev_r).wait_send()
        to_x(q, x, 1, dev_l).wait_send()
        relay(q, xl, 0, dev_r).wait_send()
        relay(q, xr, 1, dev_l).wait_send()
        for n in range(4):
            to_sib(q, n).wait_send()
    for copy in outs:
        copy.wait()


def body(Z, Y, X, hidden, w_dkv, kv_gain, queries, w_uk, w_uv, store, page_table, cached_len, app_len):
    rows = hidden.shape[0]
    heads = w_uk.shape[1] // NOPE
    G = Z * Y
    KC = Z // 2
    n_ph = len(PHASES)
    any_spec = pl.BlockSpec(memory_space=pl.ANY)
    smem = pl.BlockSpec(memory_space=pltpu.SMEM)
    vmem = pl.BlockSpec(memory_space=pltpu.VMEM)
    hrows = rows // 2
    traj = heads * APP
    widest = MAXP * max(PHASES)
    VM, DMA = pltpu.VMEM, pltpu.SemaphoreType.DMA
    return pl.pallas_call(
        functools.partial(kernel, Z, Y, X),
        out_shape=jax.ShapeDtypeStruct((rows, heads * VHEAD), bf16),
        in_specs=[smem, smem, smem, vmem] + [any_spec] * 6,
        out_specs=any_spec,
        scratch_shapes=[
            VM(store.shape, bf16),
            VM(hidden.shape, bf16),
            VM((KVW, hidden.shape[1]), bf16),
            VM(queries.shape, bf16),
            VM(w_uk.shape, bf16),
            VM(w_uv.shape, bf16),
            VM((TR_G, traj, KVW), bf16),
            VM((rows, KVW), f32),
            VM((hrows, KVW), f32),
            VM((hrows, KVW), f32),
            VM((3, hrows // X, KVW), f32),
            VM((rows, KVW), bf16),
            VM((TR_G, traj, 128), f32),
            VM((TR_G, traj, 128), f32),
            VM((TR_G, traj, LAT), f32),
            VM((traj, widest), f32),
            VM((traj, widest), f32),
            VM((traj, widest), bf16),
            VM((widest, KVW), bf16),
            VM((widest, KVW), bf16),
            VM((heads, rows, LAT), bf16),
            VM((rows, heads * VHEAD), bf16),
            DMA((6,)),
            DMA((4,)),
            DMA((n_ph, KC)),
            DMA((n_ph, KC)),
            DMA((n_ph, 2)),
            DMA((n_ph, 2)),
            DMA((n_ph, 2)),
            DMA((n_ph, 2)),
            DMA((n_ph, 4)),
            DMA((n_ph, 4)),
            DMA((8,)),
            DMA((8,)),
        ]
        + [VM((KC, width, KVW), bf16) for width in PHASES]
        + [VM((G, width, KVW), bf16) for width in PHASES],
        compiler_params=pltpu.CompilerParams(
            collective_id=0, has_side_effects=True, vmem_limit_bytes=60 * 1024 * 1024
        ),
        name="resume",
    )(page_table.T, cached_len, app_len, kv_gain[None, :], hidden, w_dkv.T, queries, w_uk, w_uv, store)


def solution(mesh):
    X = mesh.shape["tp"] // 2
    Y = X
    Z = mesh.shape["grp"] // Y
    in_specs = (
        P("grp", "tp"),
        P("tp", None),
        P(),
        P("grp", "tp"),
        P(None, "tp"),
        P(None, "tp"),
        P("grp", None, None),
        P(),
        P(),
        P(),
    )
    return jax.shard_map(
        functools.partial(body, Z, Y, X), mesh=mesh, in_specs=in_specs, out_specs=P("grp", "tp"), check_vma=False
    )
```

time: 210 us -> 59.7 us (0.28)
  the two profiles are of different devices: /device:TPU:15 before, /device:TPU:1 now
where the time goes in v2:
time: 59.7 us; the launch traced here: 59.6 us
  Pallas kernels  57.2 us (96%)
  local copies, waits for them, and re-layouts  2.3 us (4%)
    pallas_call x1, Pallas kernels, body(): pl.pallas_call(functools.partial(kernel, Z, Y, X), out_shape=jax.ShapeDty...  57.2 us
    unnamed x1, local copies, waits for them, and re-layouts  2.3 us

profile of v2, /device:TPU:1, one launch (start us, length us, event | category | flops | bytes accessed | tf_op | source)
XLA Modules:
  0.0 59.6 jit_solution(470180587421981823)
XLA Ops:
  0.0 57.2 %resume.1 = bf16[256,2048]{1,0:T(8,128)(2,1)} custom-call(s32[8,128]{1,0:T(8,128)} %bitcast.4, s32[128]{0:T(128)} %len_ref.1, s32[128]{0:T(128)} %app_ref.1, f32[1,512]{1,0:T(1,128)} %bitcast.5, bf16[256,896]{1,0:T(8,128)(2,1)} %hidden_hbm.1, bf16[576,896]{1,0:T(8,128)(2,1)} %bitcast.3, bf16[256,3072]{1,0:T(8,128)(2,1)} %queries_hbm.1, ...), custom_call_target="tpu_custom_call" | custom-call | tf_op jit(solution)/shard_map/resume/pallas_call | solution.py:389
  57.3 2.3 %copy.12 = bf16[256,2048]{1,0:T(8,128)(2,1)} copy(bf16[256,2048]{1,0:T(8,128)(2,1)} %resume.1) | data formatting | bytes 2097152

commit v3 on v2

--- a/solution.py
+++ b/solution.py
@@ -22,6 +22,10 @@
 NT = (((1,), (1,)), ((), ()))
 PHASES = (32, 32, 32, 32)
 CHUNK = 128
+GATHER = 3
+DIRECT = (((0, 0), (0, 1), (0, 2), (1, 0)), ((0, 3), (7, 0), (1, 1), (7, 3)))
+NDIR = len(DIRECT[0])
+SIDE = NDIR + 4 * GATHER
 SCALE = math.log2(math.e) / math.sqrt(NOPE + ROPE)
 bf16, f32 = jnp.bfloat16, jnp.float32
 
@@ -48,18 +52,17 @@
 def kernel(
     Z, Y, X,
     pt_ref, len_ref, app_ref, gain_ref, hidden_hbm, wdkv_hbm, queries_hbm, wuk_hbm, wuv_hbm, store_hbm,
-    out_hbm,
+    out_v,
     *scratch,
 ):
     n_ph = len(PHASES)
     (store_v, hidden, wdkv, queries, wuk, wuv, q_v, kv_part, kv_half, kv_sib, kv_in, fresh,
-     m_ref, l_ref, acc_ref, s_a, s_b, p_ref, kt_a, kt_b, o_ref, out_v,
-     load_sem, out_sem, send1, recv1, sendx, recvx, sendr, recvr, sends, recvs, kvsend, kvrecv) = scratch[: -2 * n_ph]
+     m_ref, l_ref, acc_ref, s_a, s_b, p_ref, kt_a, kt_b, o_ref,
+     load_sem, send1, recv1, sendx, recvx, sendr, recvr, sends, recvs, kvsend, kvrecv) = scratch[: -2 * n_ph]
     stage = scratch[-2 * n_ph : -n_ph]
     pages = scratch[-n_ph:]
     s_refs, kts = (s_a, s_b), (kt_a, kt_b)
     G = Z * Y
-    KC = Z // 2
     g = lax.axis_index("grp")
     tp = lax.axis_index("tp")
     z, y = g // Y, lax.rem(g, Y)
@@ -75,24 +78,35 @@
              (wuk_hbm, wuk), (wuv_hbm, wuv))
         )
     ]
-    for load in loads:
-        load.start()
+    for i in (1, 2, 0):
+        loads[i].start()
 
     xr, xl, xo = rem(x + 1, X), rem(x - 1, X), rem(x + 2, X)
     dev_r, dev_l, dev_o, dev_s = (
         (g, xr * 2 + c), (g, xl * 2 + c), (g, xo * 2 + c), (g, x * 2 + 1 - c)
     )
-    is_self = (x == 0) & (c == 0)
-
-    def remote(k, fn):
-        if k == 0:
-            pl.when(jnp.logical_not(is_self))(fn)
+
+    def gathered(k):
+        dz = jnp.where(c == 0, 2 + 2 * k, (3, 5, jnp.where(x < 2, 1, Z - 1))[k])
+        dy = lax.rem(dz + x, Y)
+        if k == 2:
+            dy = jnp.where(c == 0, dy, jnp.where(x < 2, 2 + x, x - 1))
+        return dz, dy
+
+    def direct(j):
+        zero, one = DIRECT[0][j], DIRECT[1][j]
+        return jnp.where(c == 0, zero[0], one[0]), jnp.where(c == 0, zero[1], one[1])
+
+    def remote(j, fn):
+        if j == GATHER:
+            pl.when(c == 1)(fn)
         else:
             fn()
 
-    def group(k, way):
-        dz = 2 * k + c
-        dy = lax.rem(dz + x, Y)
+    moves = [gathered(k) for k in range(GATHER)] + [direct(j) for j in range(len(DIRECT[0]))]
+
+    def group(n, way):
+        dz, dy = moves[n]
         return rem(z + way * dz, Z) * Y + rem(y + way * dy, Y)
 
     barrier = pltpu.get_barrier_semaphore()
@@ -102,8 +116,21 @@
 
     for dev in (dev_r, dev_l, dev_o, dev_s):
         greet(dev)
-    for k in range(KC):
-        remote(k, lambda: greet((group(k, -1), tp)))
+    for n in range(len(moves)):
+        remote(n, lambda: greet((group(n, -1), tp)))
+
+    def slot_of(t, m):
+        source = pt_ref[m, g * TR_G + t] // G
+        dz = rem(z - source // Y, Z)
+        dy = rem(y - lax.rem(source, Y), Y)
+        who = lax.rem(dy - dz + Z, Y)
+        gather = jnp.where(lax.rem(dz, 2) == 0, NDIR, SIDE + NDIR) + who * GATHER + dz // 2 - 1
+        same = jnp.where(dy == 3, SIDE, dy)
+        after = jnp.where(dy == 0, 3, jnp.where(dy == 1, SIDE + 2, SIDE + NDIR + (dy - 2) * GATHER + 2))
+        ahead = jnp.where(dy == 0, SIDE + 1, jnp.where(dy == 3, SIDE + 3, SIDE + NDIR + (dy + 1) * GATHER + 2))
+        return jnp.where(dz == 0, same, jnp.where(dz == 1, after, jnp.where(dz == Z - 1, ahead, gather)))
+
+    places = [[slot_of(t, m) for m in range(MAXP)] for t in range(TR_G)]
 
     def find(dest):
         found = jnp.int32(0)
@@ -113,76 +140,34 @@
                 found = found + jnp.where(value // G == g, lax.rem(value, G), 0)
         return found
 
-    picks = [find(group(k, 1)) for k in range(KC)]
+    picks = [find(group(n, 1)) for n in range(len(moves))]
 
     def rcopy(src, dst, ss, rs, dev):
         return pltpu.make_async_remote_copy(
             src_ref=src, dst_ref=dst, send_sem=ss, recv_sem=rs, device_id=dev, device_id_type=MESH
         )
 
-    def slot(who):
-        return c * (X * KC) + who * KC
-
-    def first(q, k):
-        return rcopy(stage[q].at[k], pages[q].at[slot(x) + k], send1.at[q, k], recv1.at[q, k], (group(k, 1), tp))
-
-    loads[0].wait()
-    for k in range(KC):
-        page = store_v[picks[k]]
+    def some(q, ref, first_slot, count):
+        return ref.at[pl.ds(2 * first_slot, 2 * count)]
+
+    def mine(who):
+        return c * SIDE + NDIR + who * GATHER
+
+    def first(q, n):
+        at = mine(x) + n if n < GATHER else c * SIDE + n - GATHER
+        return rcopy(
+            some(q, stage[q], n, 1), some(q, pages[q], at, 1), send1.at[q, n], recv1.at[q, n], (group(n, 1), tp)
+        )
+
+    def prepare(n):
+        page = store_v[picks[n]]
         lat, rope = page[0:LAT, :].T, page[LAT:KVW, :].T
         for q in range(n_ph):
-            stage[q][k, :, 0:LAT] = lat[starts[q] : starts[q] + PHASES[q], :]
-            stage[q][k, :, LAT:KVW] = rope[starts[q] : starts[q] + PHASES[q], :]
-
-    @pl.when(is_self)
-    def _():
-        for q in range(n_ph):
-            pages[q][0] = stage[q][0]
-
-    pl.semaphore_wait(barrier, KC + 4 - is_self.astype(jnp.int32))
-    for q in range(n_ph):
-        for k in reversed(range(KC)):
-            remote(k, lambda: first(q, k).start())
-
-    def to_x(q, who, n, dev):
-        part = pages[q].at[pl.ds(slot(who), KC)]
-        return rcopy(part, part, sendx.at[q, n], recvx.at[q, n], dev)
-
-    def relay(q, who, n, dev):
-        part = pages[q].at[pl.ds(slot(who) + n * (KC // 2), KC // 2)]
-        return rcopy(part, part, sendr.at[q, n], recvr.at[q, n], dev)
-
-    def to_sib(q, n):
-        part = pages[q].at[pl.ds(slot((x, xl, xr, xo)[n]), KC)]
-        return rcopy(part, part, sends.at[q, n], recvs.at[q, n], dev_s)
-
-    def from_sib(q, n):
-        part = pages[q].at[pl.ds((1 - c) * (X * KC) + (x, xl, xr, xo)[n] * KC, KC)]
-        return rcopy(part, part, sends.at[q, n], recvs.at[q, n], dev_s)
-
-    def step_own(q):
-        for k in range(KC):
-            remote(k, lambda: first(q, k).wait_recv())
-        to_x(q, x, 0, dev_r).start()
-        to_x(q, x, 1, dev_l).start()
-        to_sib(q, 0).start()
-
-    def step_side(q):
-        to_x(q, xl, 0, dev_r).wait_recv()
-        relay(q, xl, 0, dev_r).start()
-        to_sib(q, 1).start()
-        to_x(q, xr, 1, dev_l).wait_recv()
-        relay(q, xr, 1, dev_l).start()
-        to_sib(q, 2).start()
-
-    def step_far(q):
-        relay(q, xo, 0, dev_r).wait_recv()
-        relay(q, xo, 1, dev_l).wait_recv()
-        to_sib(q, 3).start()
-
-    def step_done(q):
-        for n in range(4):
-            from_sib(q, n).wait_recv()
+            for e in range(2):
+                unit = PHASES[q] // 2
+                part = slice(starts[q] + e * unit, starts[q] + (e + 1) * unit)
+                stage[q][2 * n + e, :, 0:LAT] = lat[part, :]
+                stage[q][2 * n + e, :, LAT:KVW] = rope[part, :]
 
     hrows = rows // 2
     brows = hrows // X
@@ -200,12 +185,6 @@
     ]
     half = fresh.at[pl.ds(c * hrows, hrows)]
     fr_s = rcopy(half, half, kvsend.at[7], kvrecv.at[7], dev_s)
-
-    def kv_one():
-        loads[1].wait()
-        loads[2].wait()
-        kv_part[...] = lax.dot_general(hidden[...], wdkv[...], NT, preferred_element_type=f32)
-        sib_kv.start()
 
     def kv_two():
         sib_kv.wait()
@@ -231,6 +210,85 @@
         for copy in fr_x:
             copy.wait()
         fr_s.start()
+
+    loads[1].wait()
+    loads[2].wait()
+    kv_part[...] = lax.dot_general(hidden[...], wdkv[...], NT, preferred_element_type=f32)
+    loads[0].wait()
+    for load in loads[3:]:
+        load.start()
+    for n in range(GATHER):
+        prepare(n)
+    pl.semaphore_wait(barrier, len(moves) + 3 + c)
+    sib_kv.start()
+    for n in range(GATHER):
+        first(0, n).start()
+    kv_two()
+    for n in range(GATHER, len(moves)):
+        prepare(n)
+    for q in range(1, n_ph + 1):
+        if q < n_ph:
+            for n in range(GATHER):
+                first(q, n).start()
+        for n in range(GATHER, len(moves)):
+            remote(n, lambda: first(q - 1, n).start())
+
+    @pl.when(c == 0)
+    def _():
+        for q in range(n_ph):
+            for e in range(2):
+                pages[q][e] = stage[q][2 * GATHER + e]
+
+    def to_x(q, who, n, dev):
+        part = some(q, pages[q], mine(who), GATHER)
+        return rcopy(part, part, sendx.at[q, n], recvx.at[q, n], dev)
+
+    def relay(q, who, n, dev):
+        part = pages[q].at[pl.ds(2 * mine(who) + n * GATHER, GATHER)]
+        return rcopy(part, part, sendr.at[q, n], recvr.at[q, n], dev)
+
+    def shared(q, n, cls):
+        if n == 4:
+            return some(q, pages[q], cls * SIDE, NDIR)
+        return some(q, pages[q], cls * SIDE + NDIR + (x, xl, xr, xo)[n] * GATHER, GATHER)
+
+    def to_sib(q, n):
+        part = shared(q, n, c)
+        return rcopy(part, part, sends.at[q, n], recvs.at[q, n], dev_s)
+
+    def from_sib(q, n):
+        part = shared(q, n, 1 - c)
+        return rcopy(part, part, sends.at[q, n], recvs.at[q, n], dev_s)
+
+    def step_own(q):
+        for n in range(GATHER):
+            first(q, n).wait_recv()
+        to_x(q, x, 0, dev_r).start()
+        to_x(q, x, 1, dev_l).start()
+        to_sib(q, 0).start()
+
+    def step_direct(q):
+        for n in range(GATHER, len(moves)):
+            remote(n, lambda: first(q, n).wait_recv())
+        to_sib(q, 4).start()
+
+    def step_side(q):
+        to_x(q, xl, 0, dev_r).wait_recv()
+        relay(q, xl, 0, dev_r).start()
+        to_sib(q, 1).start()
+        to_x(q, xr, 1, dev_l).wait_recv()
+        relay(q, xr, 1, dev_l).start()
+        to_sib(q, 2).start()
+
+    def step_far(q):
+        relay(q, xo, 0, dev_r).wait_recv()
+        relay(q, xo, 1, dev_l).wait_recv()
+        to_sib(q, 3).start()
+
+    def step_done(q):
+        step_direct(q)
+        for n in range(5):
+            from_sib(q, n).wait_recv()
 
     def q_heads(first_head, last_head, angles):
         cosine, sine = angles
@@ -263,11 +321,9 @@
     def scores(q, t, b):
         width = PHASES[q]
         for m in range(MAXP):
-            source = pt_ref[m, g * TR_G + t] // G
-            dz = rem(z - source // Y, Z)
-            dy = rem(y - lax.rem(source, Y), Y)
-            at = lax.rem(dz, 2) * (X * KC) + lax.rem(dy - dz + 2 * Z * Y, Y) * KC + dz // 2
-            kts[b][m * width : (m + 1) * width, :] = pages[q][at]
+            for e in range(2):
+                at = m * width + e * (width // 2)
+                kts[b][at : at + width // 2, :] = pages[q][2 * places[t][m] + e]
         n = MAXP * width
         s_refs[b][:, 0:n] = lax.dot_general(q_v[t], kts[b][0:n, :], NT, preferred_element_type=f32)
 
@@ -300,48 +356,48 @@
             o = (acc_ref[t, r : r + CHUNK, :] * (1.0 / total)).astype(bf16)
             o_ref[r // APP : (r + CHUNK) // APP, t * APP : (t + 1) * APP, :] = o.reshape(CHUNK // APP, APP, LAT)
 
-    kv_one()
     tok = lax.broadcasted_iota(jnp.int32, (APP, 1), 0)
     pos = jnp.concatenate([tok + len_ref[g * TR_G + t] for t in range(TR_G)], axis=0)
     angles = tables(pos, ROPE)
-    kv_two()
     loads[3].wait()
     loads[4].wait()
     q_heads(0, heads // 2, angles)
-    step_own(0)
     kv_three()
     q_heads(heads // 2, heads, angles)
+    step_own(0)
+    kv_four()
     step_own(1)
-    kv_four()
     step_side(0)
-    step_own(2)
     fr_s.wait()
     start_softmax(0)
+    step_own(2)
     start_softmax(1)
     step_far(0)
     step_side(1)
     start_softmax(2)
     start_softmax(3)
-    step_own(3)
 
     before = {
-        (0, 0): [(step_done, 0)],
+        (0, 0): [(step_done, 0), (step_own, 3)],
         (0, 2): [(step_far, 1), (step_side, 2)],
         (1, 0): [(step_done, 1)],
-        (1, 1): [(step_far, 2)],
-        (1, 2): [(step_side, 3)],
+        (1, 2): [(step_far, 2), (step_side, 3)],
         (2, 0): [(step_done, 2)],
         (2, 2): [(step_far, 3)],
         (3, 0): [(step_done, 3)],
     }
     units = [(q, t) for q in range(n_ph) for t in range(TR_G)]
     for i, (q, t) in enumerate(units):
-        for step, arg in before.get((q, t), ()):
+        steps = before.get((q, t), ())
+        if i > 0 and steps:
+            combine(*units[i - 1], (i - 1) % 2)
+        for step, arg in steps:
             step(arg)
         scores(q, t, i % 2)
         if i > 0:
             pq, pt = units[i - 1]
-            combine(pq, pt, (i - 1) % 2)
+            if not steps:
+                combine(pq, pt, (i - 1) % 2)
             if pq == n_ph - 1:
                 finish(pt)
     combine(*units[-1], (len(units) - 1) % 2)
@@ -349,35 +405,25 @@
 
     loads[5].wait()
     valid = jnp.concatenate([tok < app_ref[g * TR_G + t] for t in range(TR_G)], axis=0)
-    outs = []
     for part in range(4):
         for h in range(part * heads // 4, (part + 1) * heads // 4):
             o = jnp.dot(o_ref[h], wuv[:, h * VHEAD : (h + 1) * VHEAD], preferred_element_type=f32)
             out_v[:, h * VHEAD : (h + 1) * VHEAD] = jnp.where(valid, o, 0.0).astype(bf16)
-        wide = heads * VHEAD // 4
-        at = pl.ds(part * wide, wide)
-        copy = pltpu.make_async_copy(out_v.at[:, at], out_hbm.at[:, at], out_sem.at[part])
-        copy.start()
-        outs.append(copy)
-
     for q in range(n_ph):
-        for k in range(KC):
-            remote(k, lambda: first(q, k).wait_send())
+        for n in range(len(moves)):
+            remote(n, lambda: first(q, n).wait_send())
         to_x(q, x, 0, dev_r).wait_send()
         to_x(q, x, 1, dev_l).wait_send()
         relay(q, xl, 0, dev_r).wait_send()
         relay(q, xr, 1, dev_l).wait_send()
-        for n in range(4):
+        for n in range(5):
             to_sib(q, n).wait_send()
-    for copy in outs:
-        copy.wait()
 
 
 def body(Z, Y, X, hidden, w_dkv, kv_gain, queries, w_uk, w_uv, store, page_table, cached_len, app_len):
     rows = hidden.shape[0]
     heads = w_uk.shape[1] // NOPE
     G = Z * Y
-    KC = Z // 2
     n_ph = len(PHASES)
     any_spec = pl.BlockSpec(memory_space=pl.ANY)
     smem = pl.BlockSpec(memory_space=pltpu.SMEM)
@@ -388,9 +434,9 @@
     VM, DMA = pltpu.VMEM, pltpu.SemaphoreType.DMA
     return pl.pallas_call(
         functools.partial(kernel, Z, Y, X),
-        out_shape=jax.ShapeDtypeStruct((rows, heads * VHEAD), bf16),
+        out_shape=pltpu.VMEM((rows, heads * VHEAD), bf16),
         in_specs=[smem, smem, smem, vmem] + [any_spec] * 6,
-        out_specs=any_spec,
+        out_specs=vmem,
         scratch_shapes=[
             VM(store.shape, bf16),
             VM(hidden.shape, bf16),
@@ -413,22 +459,20 @@
             VM((widest, KVW), bf16),
             VM((widest, KVW), bf16),
             VM((heads, rows, LAT), bf16),
-            VM((rows, heads * VHEAD), bf16),
             DMA((6,)),
-            DMA((4,)),
-            DMA((n_ph, KC)),
-            DMA((n_ph, KC)),
+            DMA((n_ph, GATHER + NDIR)),
+            DMA((n_ph, GATHER + NDIR)),
             DMA((n_ph, 2)),
             DMA((n_ph, 2)),
             DMA((n_ph, 2)),
             DMA((n_ph, 2)),
-            DMA((n_ph, 4)),
-            DMA((n_ph, 4)),
+            DMA((n_ph, 5)),
+            DMA((n_ph, 5)),
             DMA((8,)),
             DMA((8,)),
         ]
-        + [VM((KC, width, KVW), bf16) for width in PHASES]
-        + [VM((G, width, KVW), bf16) for width in PHASES],
+        + [VM((2 * (GATHER + NDIR), width // 2, KVW), bf16) for width in PHASES]
+        + [VM((2 * G, width // 2, KVW), bf16) for width in PHASES],
         compiler_params=pltpu.CompilerParams(
             collective_id=0, has_side_effects=True, vmem_limit_bytes=60 * 1024 * 1024
         ),

time: 59.7 us -> 57.4 us (0.961)
  local copies, waits for them, and re-layouts: 2.3 us -> 0.97 us
  Pallas kernels: 57.2 us -> 56.3 us
    unnamed x1, local copies, waits for them, and re-layouts: 2.3 us -> 0.97 us
    pallas_call x1, Pallas kernels: 57.2 us -> 56.3 us  [body(): pl.pallas_call(functools.partial(kernel, Z, Y, X), out_shape=pltpu.VMEM((...]
where the time goes in v3:
time: 57.4 us; the launch traced here: 57.3 us
  Pallas kernels  56.3 us (98%)
  local copies, waits for them, and re-layouts  0.97 us (2%)
    pallas_call x1, Pallas kernels, body(): pl.pallas_call(functools.partial(kernel, Z, Y, X), out_shape=pltpu.VMEM((...  56.3 us

profile of v3, /device:TPU:1, one launch (start us, length us, event | category | flops | bytes accessed | tf_op | source)
XLA Modules:
  0.0 57.3 jit_solution(17744162806090727509)
XLA Ops:
  0.0 56.3 %resume.1 = bf16[256,2048]{1,0:T(8,128)(2,1)S(1)} custom-call(s32[8,128]{1,0:T(8,128)} %bitcast.4, s32[128]{0:T(128)} %len_ref.1, s32[128]{0:T(128)} %app_ref.1, f32[1,512]{1,0:T(1,128)} %bitcast.5, bf16[256,896]{1,0:T(8,128)(2,1)} %hidden_hbm.1, bf16[576,896]{1,0:T(8,128)(2,1)} %bitcast.3, bf16[256,3072]{1,0:T(8,128)(2,1)} %queries_hbm.1, ...), custom_call_target="tpu_custom_call" | custom-call | tf_op jit(solution)/shard_map/resume/pallas_call | solution.py:435
  56.3 1.0 %copy.12 = bf16[256,2048]{1,0:T(8,128)(2,1)} copy(bf16[256,2048]{1,0:T(8,128)(2,1)S(1)} %resume.1) | data formatting | bytes 2097152

commit v4 on v3

--- a/solution.py
+++ b/solution.py
@@ -379,11 +379,11 @@
 
     before = {
         (0, 0): [(step_done, 0), (step_own, 3)],
-        (0, 2): [(step_far, 1), (step_side, 2)],
+        (0, 1): [(step_far, 1), (step_side, 2)],
         (1, 0): [(step_done, 1)],
-        (1, 2): [(step_far, 2), (step_side, 3)],
+        (1, 1): [(step_far, 2), (step_side, 3)],
         (2, 0): [(step_done, 2)],
-        (2, 2): [(step_far, 3)],
+        (2, 1): [(step_far, 3)],
         (3, 0): [(step_done, 3)],
     }
     units = [(q, t) for q in range(n_ph) for t in range(TR_G)]

time: 57.4 us -> 59.5 us (1.037)
  Pallas kernels: 56.3 us -> 58.4 us
    pallas_call x1, Pallas kernels: 56.3 us -> 58.4 us  [body(): pl.pallas_call(functools.partial(kernel, Z, Y, X), out_shape=pltpu.VMEM((...]
where the time goes in v4:
time: 59.5 us; the launch traced here: 59.4 us
  Pallas kernels  58.4 us (98%)
  local copies, waits for them, and re-layouts  0.97 us (2%)
    pallas_call x1, Pallas kernels, body(): pl.pallas_call(functools.partial(kernel, Z, Y, X), out_shape=pltpu.VMEM((...  58.4 us

profile of v4, /device:TPU:1, one launch (start us, length us, event | category | flops | bytes accessed | tf_op | source)
XLA Modules:
  0.0 59.4 jit_solution(17332036953075903745)
XLA Ops:
  0.0 58.4 %resume.1 = bf16[256,2048]{1,0:T(8,128)(2,1)S(1)} custom-call(s32[8,128]{1,0:T(8,128)} %bitcast.4, s32[128]{0:T(128)} %len_ref.1, s32[128]{0:T(128)} %app_ref.1, f32[1,512]{1,0:T(1,128)} %bitcast.5, bf16[256,896]{1,0:T(8,128)(2,1)} %hidden_hbm.1, bf16[576,896]{1,0:T(8,128)(2,1)} %bitcast.3, bf16[256,3072]{1,0:T(8,128)(2,1)} %queries_hbm.1, ...), custom_call_target="tpu_custom_call" | custom-call | tf_op jit(solution)/shard_map/resume/pallas_call | solution.py:435
  58.4 1.0 %copy.12 = bf16[256,2048]{1,0:T(8,128)(2,1)} copy(bf16[256,2048]{1,0:T(8,128)(2,1)S(1)} %resume.1) | data formatting | bytes 2097152
